TPU v7x, 256 devices: a whole 4x4x8 slice. The times are simulated.
256 devices in a mesh: chan: 16 (over z_lo, y), freq: 16 (over z_hi, x, core).
Axes of the slice: x: 4, y: 4, z: 8 (z_hi: 2, z_lo: 4; z = z_hi * 4 + z_lo), core: 2. Of those that a mesh axis runs over, the one named last changes fastest.
Arguments:
- traces: bfloat16 [64, 2048, 2048], P('freq', 'chan'), may hold values from -6 to 6
Outputs:
- correlations: bfloat16 [64, 2048, 2048], P('freq', 'chan')
All inputs are finite; a program needn't handle non-finite values.
Results may differ from a plain program's by a relative error of at most 0.0076.
Values may be sent and summed in bfloat16 or wider, within the bound.
A program may use at most 128 MiB of HBM per device.

v0:
```python
import math

import jax
import jax.numpy as jnp
from jax import lax
from jax.sharding import PartitionSpec as P

K = 64


def from_behind(block, axis, distance):
    devices = range(lax.axis_size(axis))
    route = [(i - distance, i) for i in devices if i - distance in devices]
    return lax.ppermute(block, axis, route)


def block_freqs(column, block_width):
    block_id = column // (2 * block_width)
    part_id = column // block_width % 2
    within = column % block_width
    return (block_id * block_width + within, part_id)


def forward_table(samples, block_width):
    columns = jnp.arange(samples, dtype=jnp.int32)
    freq_of, part_of = block_freqs(columns, block_width)
    sample_idx = jnp.arange(samples, dtype=jnp.int32)
    phases = sample_idx[:, None] * freq_of[None, :] % samples
    angles = 2.0 * math.pi / samples * phases.astype(jnp.float32)
    values = jnp.where(part_of[None, :] == 0, jnp.cos(angles), -jnp.sin(angles))
    return values.astype(jnp.bfloat16)


def inverse_table(samples, block_width):
    rows_idx = jnp.arange(samples, dtype=jnp.int32)
    freq_of, part_of = block_freqs(rows_idx, block_width)
    lag_idx = jnp.arange(samples, dtype=jnp.int32) - samples // 2
    phases = jnp.mod(freq_of[:, None] * lag_idx[None, :], samples)
    angles = 2.0 * math.pi / samples * phases.astype(jnp.float32)
    factor = 1.0 / math.sqrt(samples // 2)
    values = jnp.where(part_of[:, None] == 0, jnp.cos(angles) * factor, -jnp.sin(angles) * factor)
    return values.astype(jnp.bfloat16)


def per_device(traces):
    windows, channels, samples = traces.shape
    half_len = samples // 2
    groups = lax.axis_size("freq")
    block_width = half_len // groups
    dft_table = forward_table(samples, block_width)
    spectra = jnp.dot(
        traces.reshape(windows * channels, samples), dft_table, preferred_element_type=jnp.float32
    )
    spectra = spectra.reshape(windows, channels, groups, 2, block_width)
    energy = spectra[:, :, :, 0] * spectra[:, :, :, 0] + spectra[:, :, :, 1] * spectra[:, :, :, 1]
    water_level = 0.1 * jnp.mean(energy, axis=(2, 3), keepdims=True)
    inverse_norm = 1.0 / jnp.sqrt(energy + water_level + 1e-06)
    whitened = (
        (spectra * inverse_norm[:, :, :, None, :])
        .astype(jnp.bfloat16)
        .reshape(windows, channels, 2 * half_len)
    )
    rim_rows = from_behind(whitened[:, :K], "chan", -1)
    extended = jnp.concatenate([whitened, rim_rows], axis=1)
    regrouped = lax.all_to_all(extended, "freq", split_axis=2, concat_axis=0, tiled=True)
    total_windows = regrouped.shape[0]
    span = channels + K
    right_side = regrouped.reshape(total_windows, span, 2, block_width)
    own_part = right_side[:, :channels]
    swapped = jnp.stack([own_part[:, :, 1], -own_part[:, :, 0]], axis=2)
    left_side = jnp.stack([own_part, swapped], axis=3)
    gram = jnp.einsum("wcpqf,wjpf->cjqf", left_side, right_side, preferred_element_type=jnp.float32)
    gram = gram.reshape(channels * span, 2 * block_width)
    gram = jnp.pad(gram, ((0, channels), (0, 0))).reshape(channels, span + 1, 2 * block_width)
    band = gram[:, 1 : K + 1]
    norm_factor = 1.0 / math.sqrt(total_windows)
    stacked = (jnp.transpose(band, (1, 0, 2)) * norm_factor).astype(jnp.bfloat16)
    lag_table = inverse_table(samples, block_width)
    return jnp.einsum(
        "kcg,gt->kct",
        lax.all_to_all(stacked, "freq", split_axis=0, concat_axis=2, tiled=True),
        lag_table,
        preferred_element_type=jnp.float32,
    ).astype(jnp.bfloat16)


def solution(mesh):
    placed = (P("freq", "chan", None),)
    return jax.shard_map(
        per_device, mesh=mesh, in_specs=placed, out_specs=P("freq", "chan", None), check_vma=False
    )
```

profile of v0, /device:TPU:95, one launch (start us, length us, event | category | flops | bytes accessed | tf_op | source)
XLA Modules:
  0.0 492.6 jit_solution(8578822975909228589)
XLA Ops:
  0.0 0.0 copy-start
  0.0 1.6 copy-done
  1.6 70.4 %fusion.12 = f32[2048,512]{0,1:T(8,128)} fusion(bf16[512,2048]{1,0:T(8,128)(2,1)S(1)} %bitcast.48, s32[2048]{0:T(1024)S(1)} %fusion.50, pred[2048]{0:T(1024)(128)(4,1)S(1)} %fusion.47), kind=kOutput, calls=%fused_computation.21 | convolution fusion | flops 4366270464 | bytes 6301696 | tf_op jit(solution)/shard_map/dot_general | solution.py:51
  72.0 5.4 %copy.29 = f32[512,2048]{0,1:T(8,128)} copy(f32[512,2048]{1,0:T(8,128)} %bitcast.53) | data formatting | bytes 8388608 | tf_op jit(solution)/shard_map/dot_general | solution.py:51
  77.4 16.6 %reshape.126 = f32[4,128,16,2,64]{1,0,4,3,2:T(4,128)} reshape(f32[512,2048]{0,1:T(8,128)} %copy.29) | data formatting | bytes 8388608 | tf_op jit(solution)/shard_map/reshape | solution.py:54
  94.0 0.0 copy-start.2
  94.0 3.5 fusion.63
  97.5 0.0 copy-done.2
  97.5 0.8 rsqrt_bitcast_fusion
  98.3 1.6 copy.30
  99.9 5.4 %copy.31 = f32[4,128,2048]{1,2,0:T(8,128)} copy(f32[4,128,2048]{2,1,0:T(8,128)} %bitcast.54) | data formatting | bytes 8388608 | tf_op jit(solution)/shard_map/reshape | solution.py:54
  105.3 3.2 fusion.32
  108.5 1.6 copy.32
  110.1 2.4 collective-permute-start
  112.5 25.9 %collective-permute-done = bf16[4,64,2048]{2,1,0:T(8,128)(2,1)S(1)} collective-permute-done((bf16[4,64,2048]{2,1,0:T(8,128)(2,1)}, bf16[4,64,2048]{2,1,0:T(8,128)(2,1)S(1)}, u32[]{:S(2)}, u32[]{:S(2)}) %collective-permute-start) | collective-permute-done | bytes 1048608 | tf_op jit(solution)/shard_map/ppermute | solution.py:14
  138.4 1.8 copy.33
  140.1 2.4 pad_maximum_fusion
  142.5 16.0 %copy.34 = bf16[4,192,2048]{1,0,2:T(4,128)(2,1)S(1)} copy(bf16[4,192,2048]{1,2,0:T(8,128)(2,1)S(1)} %pad_maximum_fusion) | data formatting | bytes 6291456 | tf_op jit(solution)/shard_map/concatenate | solution.py:64
  158.5 107.4 %all_to_all.33 = bf16[4,192,2048]{1,0,2:T(4,128)(2,1)S(1)} all-to-all(bf16[4,192,2048]{1,0,2:T(4,128)(2,1)S(1)} %copy.34), channel_id=1, replica_groups=mesh['chan'=16,'freq'=16] {'freq'}, dimensions={2} | all-to-all | bytes 6291456 | tf_op jit(solution)/shard_map/all_to_all | solution.py:65
  266.0 0.8 copy.48
  266.8 0.5 fusion.64
  267.3 0.5 slice.35
  267.7 0.7 copy.52
  268.4 0.8 copy_negate_fusion
  269.2 2.0 maximum_bitcast_fusion
  271.3 10.4 %convolution_bitcast_fusion = f32[128,192,2,64]{0,1,2,3:T(8,128)} fusion(bf16[64,128,2,1,64]{1,0,2,3,4:T(8,128)(2,1)S(1)} %get-tuple-element.7, bf16[64,128,2,1,64]{1,0,2,3,4:T(8,128)(2,1)S(1)} %get-tuple-element.8, bf16[64,192,2,64,1]{1,3,2,0,4:T(8,128)(2,1)S(1)} %bitcast.51), kind=kOutput, calls=%fused_computation.36 | convolution fusion | flops 813694976 | bytes 19922944 | tf_op jit(solution)/shard_map/wcpqf,wjpf->cjqf/dot_general | solution.py:72
  281.7 24.4 %copy.55 = f32[128,192,2,64]{3,2,1,0:T(2,128)} copy(f32[128,192,2,64]{0,1,2,3:T(8,128)} %convolution_bitcast_fusion) | data formatting | bytes 25165824
  306.1 23.9 %reshape.133 = f32[24576,128]{1,0:T(8,128)} reshape(f32[128,192,2,64]{3,2,1,0:T(2,128)} %copy.55) | data formatting | bytes 25165824
  330.0 9.3 %pad.4.clone = f32[24704,128]{1,0:T(8,128)} pad(f32[24576,128]{1,0:T(8,128)} %reshape.133, f32[]{:T(128)} %constant.110.clone.1), padding=0_128x0_0 | pad | bytes 25231364 | tf_op jit(solution)/shard_map/jit(_pad)/pad | solution.py:74
  339.3 11.6 %reshape.129 = f32[128,193,128]{2,1,0:T(8,128)} reshape(f32[24704,128]{1,0:T(8,128)} %pad.4.clone) | data formatting | bytes 25296896 | tf_op jit(solution)/shard_map/reshape | solution.py:74
  350.9 3.0 fusion.36
  353.9 2.7 copy.43
  356.6 6.3 %all-to-all-start.1 = ((bf16[64,128,128]{2,1,0:T(8,128)(2,1)}), bf16[64,128,128]{2,1,0:T(8,128)(2,1)}, u32[]{:S(2)}, u32[]{:S(2)}) async-start(bf16[64,128,128]{2,1,0:T(8,128)(2,1)} %copy.43), calls=%async_computation.1 | async-start | bytes 4194304 | tf_op jit(solution)/shard_map/all_to_all | solution.py:81
  362.9 54.7 %all-to-all-done.1 = bf16[64,128,128]{2,1,0:T(8,128)(2,1)} async-done(((bf16[64,128,128]{2,1,0:T(8,128)(2,1)}), bf16[64,128,128]{2,1,0:T(8,128)(2,1)}, u32[]{:S(2)}, u32[]{:S(2)}) %all-to-all-start.1) | async-done | bytes 2097184 | tf_op jit(solution)/shard_map/all_to_all | solution.py:81
  417.5 0.0 copy-start.1
  417.5 74.7 %fusion.33 = bf16[4,128,2048]{2,1,0:T(8,128)(2,1)} fusion(s32[2048]{0:T(1024)S(1)} %iota_add_fusion, s32[2048]{0:T(1024)S(1)} %fusion.50, pred[2048]{0:T(1024)(128)(4,1)S(1)} %fusion.47, bf16[16,4,16,8,128]{4,3,2,1,0:T(8,128)(2,1)} %bitcast.24), kind=kOutput, calls=%fused_computation.46 | convolution fusion | flops 4375707648 | bytes 4212736 | tf_op jit(solution)/shard_map/kcg,gt->kct/dot_general | solution.py:79
  492.3 0.0 copy-done.1
  (4 shorter events, 0.0 us)
Async XLA Ops:
  0.0 1.6 copy-start
  94.0 3.5 copy-start.2
  110.1 28.2 %collective-permute-start = (bf16[4,64,2048]{2,1,0:T(8,128)(2,1)}, bf16[4,64,2048]{2,1,0:T(8,128)(2,1)S(1)}, u32[]{:S(2)}, u32[]{:S(2)}) collective-permute-start(bf16[4,64,2048]{2,1,0:T(8,128)(2,1)} %copy.32), channel_id=1, source_target_pairs={{16,0},{32,16},{48,32},{64,48},{80,64},{96,80},{112,96},{128,112},... | collective-permute-start | bytes 3145736 | tf_op jit(solution)/shard_map/ppermute | solution.py:14
  356.6 61.0 %all-to-all-start.1 = ((bf16[64,128,128]{2,1,0:T(8,128)(2,1)}), bf16[64,128,128]{2,1,0:T(8,128)(2,1)}, u32[]{:S(2)}, u32[]{:S(2)}) async-start(bf16[64,128,128]{2,1,0:T(8,128)(2,1)} %copy.43), calls=%async_computation.1 | async-start | bytes 4194304 | tf_op jit(solution)/shard_map/all_to_all | solution.py:81
  417.5 74.7 %copy-start.1 = (bf16[4,128,2048]{2,1,0:T(8,128)(2,1)S(1)}, bf16[4,128,2048]{2,1,0:T(8,128)(2,1)}, u32[]{:S(2)}) copy-start(bf16[4,128,2048]{2,1,0:T(8,128)(2,1)} %param.1) | copy-start | bytes 6291460
where the time goes:
time: 502 us; the launch traced here: 493 us
  matrix products  156 us (31%)
  local copies, waits for them, and re-layouts  124 us (25%)
  blocking collectives  107 us (21%)
  waiting for transfers between devices  80.5 us (16%)
  other arithmetic  15.7 us (3%)
  starting transfers between devices  8.66 us (2%)
    all_to_all x1, blocking collectives, per_device(): lax.all_to_all(extended, 'freq', split_axis=2, concat_axis=0, tiled=True)  107 us
    dot_general x1, matrix products, per_device(): jnp.einsum('kcg,gt->kct', lax.all_to_all(stacked, 'freq', split_axis=0, c...  74.7 us
    dot_general x1, matrix products, per_device(): jnp.dot(traces.reshape(windows * channels, samples), dft_table, preferred...  70.4 us
    all_to_all x1, waiting for transfers between devices, per_device(): lax.all_to_all(stacked, 'freq', split_axis=0, concat_axis=2, tiled=True)  54.7 us
    unnamed x9, local copies, waits for them, and re-layouts  50.6 us
    ppermute x1, waiting for transfers between devices, from_behind(): return lax.ppermute(block, axis, route)  25.9 us
    reshape x2, local copies, waits for them, and re-layouts, per_device(): spectra = spectra.reshape(windows, channels, groups, 2, block_width)  22 us
    concatenate x1, local copies, waits for them, and re-layouts, per_device(): extended = jnp.concatenate([whitened, rim_rows], axis=1)  16 us
  transfers between devices with their start and end apart: 2, of which 2 were waited for; matrix products, arithmetic and copies ran while one was open for 0% of the time, Pallas kernels for 0%

commit v1 on v0

v1 whole, which is shorter than its diff:
```python
import functools
import math

import jax
import jax.numpy as jnp
import ml_dtypes
import numpy as np
from jax import lax
from jax.experimental import pallas as pl
from jax.experimental.pallas import tpu as pltpu
from jax.sharding import PartitionSpec as P

MESH = pl.DeviceIdType.MESH
BF16 = jnp.bfloat16
F32 = jnp.float32

S = 2048
W4 = 4
N = 16
CB = 128
K = 64
STAGES = 4
FS = 64 // STAGES
GS = FS // 4
ROWS = N * 2 * FS


def table():
    stage, shard, local = np.meshgrid(np.arange(STAGES), np.arange(N), np.arange(FS), indexing="ij")
    freq = (shard * 64 + stage * FS + local)[:, :, None, :, None]
    angle = (2.0 * math.pi / S) * ((freq * np.arange(S)) % S)
    values = np.concatenate([np.cos(angle), -np.sin(angle)], axis=2)
    return values.reshape(STAGES, ROWS, S).astype(ml_dtypes.bfloat16)


def partner(me, d):
    half, x, core = me // 8, (me // 2) % 4, me % 2
    half = (half + 1 - d // 8) % 2
    x = (x + 1 + (d % 8) // 2) % 4
    core = (core + 1 + d) % 2
    return half * 8 + x * 2 + core


def kernel(
    x_hbm, tbl_hbm, o_hbm,
    x_v, tbl, sums, level, spec, mix, send1, recv1, hsend, hrecv, gram, zbuf, send2, recv2, lhs2, acc, out_v,
    x_sem, tbl_sem, s1_sem, r1_sem, l1_sem, hs_sem, hr_sem, s2_sem, r2_sem, l2_sem, o_sem,
):
    chan, me = lax.axis_index("chan"), lax.axis_index("freq")

    x_copy = pltpu.make_async_copy(x_hbm, x_v, x_sem)
    x_copy.start()
    tbl_copies = [pltpu.make_async_copy(tbl_hbm.at[s], tbl.at[s], tbl_sem.at[s]) for s in range(STAGES)]
    for copy in tbl_copies:
        copy.start()

    barrier = pltpu.get_barrier_semaphore()
    for d in range(N - 1):
        pl.semaphore_signal(barrier, inc=1, device_id=(chan, partner(me, d)), device_id_type=MESH)

    @pl.when(chan < N - 1)
    def _():
        pl.semaphore_signal(barrier, inc=1, device_id=(chan + 1, me), device_id_type=MESH)

    x_copy.wait()

    def fold(b, carry):
        rows = pl.ds(pl.multiple_of(b * 64, 64), 64)
        squares = jnp.zeros((64, 128), F32)
        plain = jnp.zeros((64, 128), F32)
        for i in range(S // 128):
            part = x_v[rows, i * 128 : (i + 1) * 128].astype(F32)
            squares += part * part
            plain += part
        sums[rows, 0:128] = squares
        sums[rows, 128:256] = plain
        return carry

    lax.fori_loop(0, W4 * CB // 64, fold, 0)
    odd = lax.broadcasted_iota(jnp.int32, (128, 128), 0) % 2
    for w in range(W4):
        squares = jnp.transpose(sums[w * CB : (w + 1) * CB, 0:128])
        plain = jnp.transpose(sums[w * CB : (w + 1) * CB, 128:256])
        even_sum = jnp.sum(jnp.where(odd == 0, plain, 0.0), axis=0, keepdims=True)
        odd_sum = jnp.sum(jnp.where(odd == 1, plain, 0.0), axis=0, keepdims=True)
        mean = jnp.sum(squares, axis=0, keepdims=True) + even_sum * odd_sum * (1.0 / 512)
        mean = 0.1 * jnp.maximum(mean, 0.0) + 1e-6
        level[:, w * CB : (w + 1) * CB] = jnp.broadcast_to(mean, (8, CB))

    pl.semaphore_wait(barrier, jnp.where(chan > 0, N, N - 1))

    def first(s, d):
        p = partner(me, d)
        return pltpu.make_async_remote_copy(
            src_ref=send1.at[s, p], dst_ref=recv1.at[s, :, :, me], send_sem=s1_sem.at[s, d], recv_sem=r1_sem.at[s, d],
            device_id=(chan, p), device_id_type=MESH,
        )

    def first_own(s):
        return pltpu.make_async_copy(send1.at[s, me], recv1.at[s, :, :, me], l1_sem.at[s])

    def rim(s):
        return pltpu.make_async_remote_copy(
            src_ref=hsend.at[s], dst_ref=hrecv.at[s], send_sem=hs_sem.at[s], recv_sem=hr_sem.at[s],
            device_id=(chan - 1, me), device_id_type=MESH,
        )

    def second(s, d):
        p = partner(me, d)
        return pltpu.make_async_remote_copy(
            src_ref=send2.at[s, p], dst_ref=recv2.at[s, :, me], send_sem=s2_sem.at[s, d], recv_sem=r2_sem.at[s, d],
            device_id=(chan, p), device_id_type=MESH,
        )

    def second_own(s):
        return pltpu.make_async_copy(send2.at[s, me], recv2.at[s, :, me], l2_sem.at[s])

    def spectra(s, carry):
        pltpu.make_async_copy(tbl_hbm.at[s], tbl.at[s], tbl_sem.at[s]).wait()
        spec[...] = lax.dot_general(
            tbl[s], x_v[...], (((1,), (1,)), ((), ())), preferred_element_type=F32
        ).reshape(N, 2, FS, W4 * CB)

        def whiten(d, carry):
            p = partner(me, d)
            real, imag = spec[p, 0], spec[p, 1]
            scale = lax.rsqrt(real * real + imag * imag + level[0:1, :])
            for part, value in enumerate((real * scale, imag * scale)):
                for w in range(W4):
                    mix[pl.ds(part * 4 * FS + w, FS, stride=4), :] = value[:, w * CB : (w + 1) * CB]
            for part in range(2):
                rows = mix[part * 4 * FS : (part + 1) * 4 * FS, :]
                send1[s, p, part] = rows.astype(BF16).reshape(GS, 16, CB)

            @pl.when(d < N - 1)
            def _():
                first(s, d).start()

            return carry

        lax.fori_loop(0, N, whiten, 0)
        first_own(s).start()
        return carry

    lax.fori_loop(0, STAGES, spectra, 0)

    @pl.when(chan == N - 1)
    def _():
        hrecv[...] = jnp.zeros_like(hrecv)

    lane = lax.broadcasted_iota(jnp.int32, (8, CB), 1)
    shift = lane + 1
    sublane = lax.broadcasted_iota(jnp.int32, (8, CB), 0)
    in_own = (sublane + shift % 8) < 8

    def pick(bit, far, near):
        rows = near.shape[0]
        mask = (shift // bit) % 2 == 1
        return jnp.where(mask[None], far.reshape(rows // 8, 8, CB), near.reshape(rows // 8, 8, CB)).reshape(rows, CB)

    def skew(g):
        g = jnp.concatenate([pick(128, g[128:192], g[0:64]), g[64:192]], axis=0)
        g = pick(64, g[64:192], g[0:128])
        g = pick(32, g[32:128], g[0:96])
        g = pick(16, g[16:96], g[0:80])
        g = pick(8, g[8:80], g[0:72])
        g = g.reshape(9, 8, CB)
        for bit in (4, 2, 1):
            mask = (shift // bit) % 2 == 1
            g = jnp.where(mask[None], pltpu.roll(g, 8 - bit, axis=1), g)
        return jnp.where(in_own[None], g[0:8], g[1:9]).reshape(64, CB)

    def middle(s, carry):
        for d in range(N - 1):
            first(s, d).wait_recv()
        first_own(s).wait()

        def pack(g, carry):
            left = recv1[s, 0, g].reshape(N * 16, CB)[:, 0:64]
            right = recv1[s, 1, g].reshape(N * 16, CB)[:, 0:64]
            hsend[s, g] = jnp.concatenate([left, right], axis=1)
            return carry

        lax.fori_loop(0, GS, pack, 0)

        @pl.when(chan > 0)
        def _():
            rim(s).start()

        @pl.when(chan < N - 1)
        def _():
            rim(s).wait_recv()

        def group(g, carry):
            real = recv1[s, 0, g].reshape(N * 16, CB)
            imag = recv1[s, 1, g].reshape(N * 16, CB)
            rim_t = jnp.transpose(hrecv[s, g])
            real_t = jnp.concatenate([jnp.transpose(real), rim_t[0:64]], axis=0)
            imag_t = jnp.concatenate([jnp.transpose(imag), rim_t[64:128]], axis=0)
            right = jnp.concatenate(
                [jnp.concatenate([real, imag], axis=1), jnp.concatenate([imag, -real], axis=1)], axis=0
            )
            left = jnp.concatenate([real_t, imag_t], axis=1)
            which = (lax.broadcasted_iota(jnp.int32, left.shape, 1) % 16) // 4
            for f in range(4):
                gram[f * 192 : (f + 1) * 192, :] = jnp.dot(
                    jnp.where(which == f, left, jnp.zeros_like(left)), right, preferred_element_type=F32
                )
            for f in range(4):
                for part in range(2):
                    zbuf[pl.ds(part * FS + g * 4 + f, K, stride=2 * FS), :] = skew(
                        gram[f * 192 : (f + 1) * 192, part * CB : (part + 1) * CB]
                    )
            return carry

        lax.fori_loop(0, GS, group, 0)

        parity = lax.broadcasted_iota(jnp.int32, (4 * 2 * FS, CB), 0) % 2
        sign = jnp.where(parity == 0, 1.0 / 256, -1.0 / 256)

        def give(d, carry):
            p = partner(me, d)
            rows = zbuf[pl.ds(pl.multiple_of(p * 8 * FS, 8 * FS), 8 * FS), :]
            send2[s, p] = (rows * sign).astype(BF16).reshape(4, 2 * FS, CB)

            @pl.when(d < N - 1)
            def _():
                second(s, d).start()

            return carry

        lax.fori_loop(0, N, give, 0)
        second_own(s).start()
        return carry

    lax.fori_loop(0, STAGES, middle, 0)

    def lags(s):
        for d in range(N - 1):
            second(s, d).wait_recv()
        second_own(s).wait()
        for k in range(4):
            lhs2[k * CB : (k + 1) * CB, :] = jnp.transpose(recv2[s, k].reshape(ROWS, CB))

        def tile(t, carry):
            columns = pl.ds(pl.multiple_of(t * 512, 512), 512)
            product = jnp.dot(lhs2[...], tbl[s, :, columns], preferred_element_type=F32)
            if s == 0:
                acc[t] = product
            elif s < STAGES - 1:
                acc[t] += product
            else:
                out_v[t] = (acc[t] + product).astype(BF16)
                pltpu.make_async_copy(out_v.at[t], o_hbm.at[:, columns], o_sem.at[t]).start()
            return carry

        lax.fori_loop(0, 4, tile, 0)

    for s in range(STAGES):
        lags(s)

    for s in range(STAGES):
        for d in range(N - 1):
            first(s, d).wait_send()
            second(s, d).wait_send()

        @pl.when(chan > 0)
        def _():
            rim(s).wait_send()

    for t in range(4):
        pltpu.make_async_copy(out_v.at[t], o_hbm.at[:, t * 512 : (t + 1) * 512], o_sem.at[t]).wait()


def per_device(traces, tbl):
    rows = W4 * CB
    dma = pltpu.SemaphoreType.DMA
    any_space = pl.BlockSpec(memory_space=pl.ANY)
    out = pl.pallas_call(
        kernel,
        out_shape=jax.ShapeDtypeStruct((rows, S), BF16),
        in_specs=[any_space, any_space],
        out_specs=any_space,
        scratch_shapes=[
            pltpu.VMEM((rows, S), BF16),
            pltpu.VMEM((STAGES, ROWS, S), BF16),
            pltpu.VMEM((rows, 256), F32),
            pltpu.VMEM((8, rows), F32),
            pltpu.VMEM((N, 2, FS, rows), F32),
            pltpu.VMEM((2 * 4 * FS, CB), F32),
            pltpu.VMEM((STAGES, N, 2, GS, 16, CB), BF16),
            pltpu.VMEM((STAGES, 2, GS, N, 16, CB), BF16),
            pltpu.VMEM((STAGES, GS, N * 16, CB), BF16),
            pltpu.VMEM((STAGES, GS, N * 16, CB), BF16),
            pltpu.VMEM((4 * 192, 256), F32),
            pltpu.VMEM((K * 2 * FS, CB), F32),
            pltpu.VMEM((STAGES, N, 4, 2 * FS, CB), BF16),
            pltpu.VMEM((STAGES, 4, N, 2 * FS, CB), BF16),
            pltpu.VMEM((4 * CB, ROWS), BF16),
            pltpu.VMEM((4, rows, 512), F32),
            pltpu.VMEM((4, rows, 512), BF16),
            dma, dma((STAGES,)),
            dma((STAGES, N)), dma((STAGES, N)), dma((STAGES,)),
            dma((STAGES,)), dma((STAGES,)),
            dma((STAGES, N)), dma((STAGES, N)), dma((STAGES,)),
            dma((4,)),
        ],
        compiler_params=pltpu.CompilerParams(collective_id=0, has_side_effects=True, vmem_limit_bytes=56 * 2**20),
        name="correlate",
    )(traces.reshape(rows, S), tbl)
    return out.reshape(traces.shape)


def solution(mesh):
    placed = P("freq", "chan", None)
    mapped = jax.shard_map(per_device, mesh=mesh, in_specs=(placed, P()), out_specs=placed, check_vma=False)
    return lambda traces: mapped(traces, jnp.asarray(table()))
```

time: 502 us -> 138 us (0.27)
  the two profiles are of different devices: /device:TPU:95 before, /device:TPU:88 now
where the time goes in v1:
time: 138 us; the launch traced here: 137 us
  Pallas kernels  134 us (97%)
  local copies, waits for them, and re-layouts  3.16 us (2%)
    pallas_call x1, Pallas kernels, per_device(): pl.pallas_call(kernel, out_shape=jax.ShapeDtypeStruct((rows, S), BF16), i...  134 us
    unnamed x1, local copies, waits for them, and re-layouts  3.16 us

profile of v1, /device:TPU:88, one launch (start us, length us, event | category | flops | bytes accessed | tf_op | source)
XLA Modules:
  0.0 137.4 jit_solution(14943089145713309941)
XLA Ops:
  0.0 134.3 %correlate.1 = bf16[512,2048]{1,0:T(8,128)(2,1)} custom-call(bf16[512,2048]{1,0:T(8,128)(2,1)} %bitcast.3, bf16[4,512,2048]{2,1,0:T(8,128)(2,1)} %constant.2.clone.tbl_hbm), custom_call_target="tpu_custom_call" | custom-call | tf_op jit(solution)/shard_map/correlate/pallas_call | solution.py:279
  134.3 3.2 %copy.4 = bf16[4,128,2048]{2,1,0:T(8,128)(2,1)} copy(bf16[4,128,2048]{2,1,0:T(8,128)(2,1)} %bitcast.2) | data formatting | bytes 4194304

commit v2 on v1

--- a/solution.py
+++ b/solution.py
@@ -42,11 +42,15 @@
 
 
 def kernel(
-    x_hbm, tbl_hbm, o_hbm,
-    x_v, tbl, sums, level, spec, mix, send1, recv1, hsend, hrecv, gram, zbuf, send2, recv2, lhs2, acc, out_v,
-    x_sem, tbl_sem, s1_sem, r1_sem, l1_sem, hs_sem, hr_sem, s2_sem, r2_sem, l2_sem, o_sem,
+    x_hbm, tbl_hbm, o_ref,
+    x_v, tbl, sums, level, spec, mix, send1, recv1, hsend, hrecv, passing, gram, zbuf, send2, recv2, lhs2, acc,
+    x_sem, tbl_sem, s1_sem, r1_sem, l1_sem, hs_sem, hr_sem, ps_sem, pr_sem, s2_sem, r2_sem, l2_sem,
 ):
     chan, me = lax.axis_index("chan"), lax.axis_index("freq")
+    depth, y = chan // 4, chan % 4
+    crossing = (y == 0) & (depth > 0)
+    relaying = (y > 0) & (depth > 0)
+    crossed = (y == 3) & (depth < 3)
 
     x_copy = pltpu.make_async_copy(x_hbm, x_v, x_sem)
     x_copy.start()
@@ -61,6 +65,15 @@
     @pl.when(chan < N - 1)
     def _():
         pl.semaphore_signal(barrier, inc=1, device_id=(chan + 1, me), device_id_type=MESH)
+
+    @pl.when(crossed)
+    def _():
+        for g in range(1, 4):
+            pl.semaphore_signal(barrier, inc=1, device_id=(chan + 1 + g, me), device_id_type=MESH)
+
+    @pl.when(relaying)
+    def _():
+        pl.semaphore_signal(barrier, inc=1, device_id=(chan - y, me), device_id_type=MESH)
 
     x_copy.wait()
 
@@ -87,7 +100,8 @@
         mean = 0.1 * jnp.maximum(mean, 0.0) + 1e-6
         level[:, w * CB : (w + 1) * CB] = jnp.broadcast_to(mean, (8, CB))
 
-    pl.semaphore_wait(barrier, jnp.where(chan > 0, N, N - 1))
+    greeted = N - 1 + jnp.where(chan > 0, 1, 0) + jnp.where(crossing, 3, 0) + jnp.where(relaying, 1, 0)
+    pl.semaphore_wait(barrier, greeted)
 
     def first(s, d):
         p = partner(me, d)
@@ -99,10 +113,22 @@
     def first_own(s):
         return pltpu.make_async_copy(send1.at[s, me], recv1.at[s, :, :, me], l1_sem.at[s])
 
-    def rim(s):
-        return pltpu.make_async_remote_copy(
-            src_ref=hsend.at[s], dst_ref=hrecv.at[s], send_sem=hs_sem.at[s], recv_sem=hr_sem.at[s],
+    def rim(s, g):
+        return pltpu.make_async_remote_copy(
+            src_ref=hsend.at[s, g], dst_ref=hrecv.at[s, g], send_sem=hs_sem.at[s, g], recv_sem=hr_sem.at[s, g],
             device_id=(chan - 1, me), device_id_type=MESH,
+        )
+
+    def to_relay(s, g):
+        return pltpu.make_async_remote_copy(
+            src_ref=hsend.at[s, g], dst_ref=passing.at[s], send_sem=hs_sem.at[s, g], recv_sem=pr_sem.at[s],
+            device_id=(chan + g, me), device_id_type=MESH,
+        )
+
+    def from_relay(s):
+        return pltpu.make_async_remote_copy(
+            src_ref=passing.at[s], dst_ref=hrecv.at[s, y], send_sem=ps_sem.at[s], recv_sem=hr_sem.at[s, y],
+            device_id=(chan - y - 1, me), device_id_type=MESH,
         )
 
     def second(s, d):
@@ -170,7 +196,7 @@
             g = jnp.where(mask[None], pltpu.roll(g, 8 - bit, axis=1), g)
         return jnp.where(in_own[None], g[0:8], g[1:9]).reshape(64, CB)
 
-    def middle(s, carry):
+    def gather(s):
         for d in range(N - 1):
             first(s, d).wait_recv()
         first_own(s).wait()
@@ -185,11 +211,29 @@
 
         @pl.when(chan > 0)
         def _():
-            rim(s).start()
-
+            rim(s, 0).start()
+
+        @pl.when(y > 0)
+        def _():
+            for g in range(1, GS):
+                rim(s, g).start()
+
+        @pl.when(crossing)
+        def _():
+            for g in range(1, GS):
+                to_relay(s, g).start()
+
+    def relay(s):
+        @pl.when(relaying)
+        def _():
+            to_relay(s, 1).wait_recv()
+            from_relay(s).start()
+
+    def products(s):
         @pl.when(chan < N - 1)
         def _():
-            rim(s).wait_recv()
+            for g in range(GS):
+                rim(s, g).wait_recv()
 
         def group(g, carry):
             real = recv1[s, 0, g].reshape(N * 16, CB)
@@ -231,9 +275,18 @@
 
         lax.fori_loop(0, N, give, 0)
         second_own(s).start()
+
+    gather(0)
+    relay(0)
+
+    def middle(s, carry):
+        gather(s)
+        relay(s)
+        products(s - 1)
         return carry
 
-    lax.fori_loop(0, STAGES, middle, 0)
+    lax.fori_loop(1, STAGES, middle, 0)
+    products(STAGES - 1)
 
     def lags(s):
         for d in range(N - 1):
@@ -250,8 +303,7 @@
             elif s < STAGES - 1:
                 acc[t] += product
             else:
-                out_v[t] = (acc[t] + product).astype(BF16)
-                pltpu.make_async_copy(out_v.at[t], o_hbm.at[:, columns], o_sem.at[t]).start()
+                o_ref[:, columns] = (acc[t] + product).astype(BF16)
             return carry
 
         lax.fori_loop(0, 4, tile, 0)
@@ -266,21 +318,23 @@
 
         @pl.when(chan > 0)
         def _():
-            rim(s).wait_send()
-
-    for t in range(4):
-        pltpu.make_async_copy(out_v.at[t], o_hbm.at[:, t * 512 : (t + 1) * 512], o_sem.at[t]).wait()
+            for g in range(GS):
+                rim(s, g).wait_send()
+
+        @pl.when(relaying)
+        def _():
+            from_relay(s).wait_send()
 
 
 def per_device(traces, tbl):
     rows = W4 * CB
     dma = pltpu.SemaphoreType.DMA
-    any_space = pl.BlockSpec(memory_space=pl.ANY)
+    any_space = pl.BlockSpec(memory_space=pltpu.HBM)
     out = pl.pallas_call(
         kernel,
-        out_shape=jax.ShapeDtypeStruct((rows, S), BF16),
+        out_shape=pltpu.VMEM((rows, S), BF16),
         in_specs=[any_space, any_space],
-        out_specs=any_space,
+        out_specs=pl.BlockSpec(memory_space=pltpu.VMEM),
         scratch_shapes=[
             pltpu.VMEM((rows, S), BF16),
             pltpu.VMEM((STAGES, ROWS, S), BF16),
@@ -292,20 +346,19 @@
             pltpu.VMEM((STAGES, 2, GS, N, 16, CB), BF16),
             pltpu.VMEM((STAGES, GS, N * 16, CB), BF16),
             pltpu.VMEM((STAGES, GS, N * 16, CB), BF16),
+            pltpu.VMEM((STAGES, N * 16, CB), BF16),
             pltpu.VMEM((4 * 192, 256), F32),
             pltpu.VMEM((K * 2 * FS, CB), F32),
             pltpu.VMEM((STAGES, N, 4, 2 * FS, CB), BF16),
             pltpu.VMEM((STAGES, 4, N, 2 * FS, CB), BF16),
             pltpu.VMEM((4 * CB, ROWS), BF16),
             pltpu.VMEM((4, rows, 512), F32),
-            pltpu.VMEM((4, rows, 512), BF16),
             dma, dma((STAGES,)),
             dma((STAGES, N)), dma((STAGES, N)), dma((STAGES,)),
-            dma((STAGES,)), dma((STAGES,)),
+            dma((STAGES, GS)), dma((STAGES, GS)), dma((STAGES,)), dma((STAGES,)),
             dma((STAGES, N)), dma((STAGES, N)), dma((STAGES,)),
-            dma((4,)),
         ],
-        compiler_params=pltpu.CompilerParams(collective_id=0, has_side_effects=True, vmem_limit_bytes=56 * 2**20),
+        compiler_params=pltpu.CompilerParams(collective_id=0, has_side_effects=True, vmem_limit_bytes=60 * 2**20),
         name="correlate",
     )(traces.reshape(rows, S), tbl)
     return out.reshape(traces.shape)

time: 138 us -> 118 us (0.86)
  the two profiles are of different devices: /device:TPU:88 before, /device:TPU:31 now
where the time goes in v2:
time: 118 us
  Pallas kernels  116 us (98%)
  local copies, waits for them, and re-layouts  1.32 us (1%)
    pallas_call x1, Pallas kernels, per_device(): pl.pallas_call(kernel, out_shape=pltpu.VMEM((rows, S), BF16), in_specs=[a...  116 us

profile of v2, /device:TPU:31, one launch (start us, length us, event | category | flops | bytes accessed | tf_op | source)
XLA Modules:
  0.0 117.7 jit_solution(14843206627649193812)
XLA Ops:
  0.0 116.3 %correlate.1 = bf16[512,2048]{1,0:T(8,128)(2,1)S(1)} custom-call(bf16[512,2048]{1,0:T(8,128)(2,1)} %bitcast.3, bf16[4,512,2048]{2,1,0:T(8,128)(2,1)} %constant.2.clone.tbl_hbm), custom_call_target="tpu_custom_call" | custom-call | tf_op jit(solution)/shard_map/correlate/pallas_call | solution.py:333
  116.4 1.3 %copy.4 = bf16[4,128,2048]{2,1,0:T(8,128)(2,1)} copy(bf16[4,128,2048]{2,1,0:T(8,128)(2,1)S(1)} %bitcast.2) | data formatting | bytes 4194304

commit v3 on v2

--- a/solution.py
+++ b/solution.py
@@ -288,19 +288,28 @@
     lax.fori_loop(1, STAGES, middle, 0)
     products(STAGES - 1)
 
-    def lags(s):
-        for d in range(N - 1):
-            second(s, d).wait_recv()
-        second_own(s).wait()
+    half = me // 8
+
+    def lags(s, sides):
+        for side in sides:
+            for d in range(8 * side, min(8 * side + 8, N - 1)):
+                second(s, d).wait_recv()
+        if 1 in sides:
+            second_own(s).wait()
+        count = 8 * len(sides) * 2 * FS
+        origin = 0 if len(sides) == 2 else (half if sides[0] == 1 else 1 - half) * 8
+        origin = origin if len(sides) == 2 else pl.multiple_of(origin, 8)
         for k in range(4):
-            lhs2[k * CB : (k + 1) * CB, :] = jnp.transpose(recv2[s, k].reshape(ROWS, CB))
+            block = recv2[s, k, pl.ds(origin, 8 * len(sides))].reshape(count, CB)
+            lhs2[k * CB : (k + 1) * CB, 0:count] = jnp.transpose(block)
 
         def tile(t, carry):
             columns = pl.ds(pl.multiple_of(t * 512, 512), 512)
-            product = jnp.dot(lhs2[...], tbl[s, :, columns], preferred_element_type=F32)
+            rows = pl.ds(pl.multiple_of(origin * 2 * FS, 2 * FS), count)
+            product = jnp.dot(lhs2[:, 0:count], tbl[s, rows, columns], preferred_element_type=F32)
             if s == 0:
                 acc[t] = product
-            elif s < STAGES - 1:
+            elif sides != (0,):
                 acc[t] += product
             else:
                 o_ref[:, columns] = (acc[t] + product).astype(BF16)
@@ -308,8 +317,10 @@
 
         lax.fori_loop(0, 4, tile, 0)
 
-    for s in range(STAGES):
-        lags(s)
+    for s in range(STAGES - 1):
+        lags(s, (0, 1))
+    lags(STAGES - 1, (1,))
+    lags(STAGES - 1, (0,))
 
     for s in range(STAGES):
         for d in range(N - 1):

time: 118 us -> 117 us (level)
  no operation moved by 1% of the time
where the time goes in v3:
time: 117 us
  Pallas kernels  116 us (99%)
  local copies, waits for them, and re-layouts  1.32 us (1%)
    pallas_call x1, Pallas kernels, per_device(): pl.pallas_call(kernel, out_shape=pltpu.VMEM((rows, S), BF16), in_specs=[a...  116 us

profile of v3, /device:TPU:31, one launch (start us, length us, event | category | flops | bytes accessed | tf_op | source)
XLA Modules:
  0.0 117.0 jit_solution(3807653238496433012)
XLA Ops:
  0.0 115.7 %correlate.1 = bf16[512,2048]{1,0:T(8,128)(2,1)S(1)} custom-call(bf16[512,2048]{1,0:T(8,128)(2,1)} %bitcast.3, bf16[4,512,2048]{2,1,0:T(8,128)(2,1)} %constant.2.clone.tbl_hbm), custom_call_target="tpu_custom_call" | custom-call | tf_op jit(solution)/shard_map/correlate/pallas_call | solution.py:344
  115.7 1.3 %copy.4 = bf16[4,128,2048]{2,1,0:T(8,128)(2,1)} copy(bf16[4,128,2048]{2,1,0:T(8,128)(2,1)S(1)} %bitcast.2) | data formatting | bytes 4194304

commit v4 on v3

--- a/solution.py
+++ b/solution.py
@@ -229,31 +229,43 @@
             to_relay(s, 1).wait_recv()
             from_relay(s).start()
 
+    def right_of(s, g):
+        real = recv1[s, 0, g].reshape(N * 16, CB)
+        imag = recv1[s, 1, g].reshape(N * 16, CB)
+        right = jnp.concatenate(
+            [jnp.concatenate([real, imag], axis=1), jnp.concatenate([imag, -real], axis=1)], axis=0
+        )
+        return real, imag, right
+
+    def multiply(g, left, right, first_row):
+        rows = left.shape[0]
+        which = (lax.broadcasted_iota(jnp.int32, left.shape, 1) % 16) // 4
+        for f in range(4):
+            gram[g, f * 192 + first_row : f * 192 + first_row + rows, :] = jnp.dot(
+                jnp.where(which == f, left, jnp.zeros_like(left)), right, preferred_element_type=F32
+            )
+
     def products(s):
+        def own(g, carry):
+            real, imag, right = right_of(s, g)
+            multiply(g, jnp.concatenate([jnp.transpose(real), jnp.transpose(imag)], axis=1), right, 0)
+            return carry
+
+        lax.fori_loop(0, GS, own, 0)
+
         @pl.when(chan < N - 1)
         def _():
             for g in range(GS):
                 rim(s, g).wait_recv()
 
         def group(g, carry):
-            real = recv1[s, 0, g].reshape(N * 16, CB)
-            imag = recv1[s, 1, g].reshape(N * 16, CB)
+            right = right_of(s, g)[2]
             rim_t = jnp.transpose(hrecv[s, g])
-            real_t = jnp.concatenate([jnp.transpose(real), rim_t[0:64]], axis=0)
-            imag_t = jnp.concatenate([jnp.transpose(imag), rim_t[64:128]], axis=0)
-            right = jnp.concatenate(
-                [jnp.concatenate([real, imag], axis=1), jnp.concatenate([imag, -real], axis=1)], axis=0
-            )
-            left = jnp.concatenate([real_t, imag_t], axis=1)
-            which = (lax.broadcasted_iota(jnp.int32, left.shape, 1) % 16) // 4
-            for f in range(4):
-                gram[f * 192 : (f + 1) * 192, :] = jnp.dot(
-                    jnp.where(which == f, left, jnp.zeros_like(left)), right, preferred_element_type=F32
-                )
+            multiply(g, jnp.concatenate([rim_t[0:64], rim_t[64:128]], axis=1), right, 128)
             for f in range(4):
                 for part in range(2):
                     zbuf[pl.ds(part * FS + g * 4 + f, K, stride=2 * FS), :] = skew(
-                        gram[f * 192 : (f + 1) * 192, part * CB : (part + 1) * CB]
+                        gram[g, f * 192 : (f + 1) * 192, part * CB : (part + 1) * CB]
                     )
             return carry
 
@@ -262,7 +274,8 @@
         parity = lax.broadcasted_iota(jnp.int32, (4 * 2 * FS, CB), 0) % 2
         sign = jnp.where(parity == 0, 1.0 / 256, -1.0 / 256)
 
-        def give(d, carry):
+        def give(i, carry):
+            d = (i % 2) * 8 + i // 2
             p = partner(me, d)
             rows = zbuf[pl.ds(pl.multiple_of(p * 8 * FS, 8 * FS), 8 * FS), :]
             send2[s, p] = (rows * sign).astype(BF16).reshape(4, 2 * FS, CB)
@@ -358,7 +371,7 @@
             pltpu.VMEM((STAGES, GS, N * 16, CB), BF16),
             pltpu.VMEM((STAGES, GS, N * 16, CB), BF16),
             pltpu.VMEM((STAGES, N * 16, CB), BF16),
-            pltpu.VMEM((4 * 192, 256), F32),
+            pltpu.VMEM((GS, 4 * 192, 256), F32),
             pltpu.VMEM((K * 2 * FS, CB), F32),
             pltpu.VMEM((STAGES, N, 4, 2 * FS, CB), BF16),
             pltpu.VMEM((STAGES, 4, N, 2 * FS, CB), BF16),

time: 117 us -> 117 us (level)
  no operation moved by 1% of the time
where the time goes in v4:
time: 117 us
  Pallas kernels  115 us (98%)
  local copies, waits for them, and re-layouts  1.32 us (1%)
    pallas_call x1, Pallas kernels, per_device(): pl.pallas_call(kernel, out_shape=pltpu.VMEM((rows, S), BF16), in_specs=[a...  115 us

profile of v4, /device:TPU:31, one launch (start us, length us, event | category | flops | bytes accessed | tf_op | source)
XLA Modules:
  0.0 116.7 jit_solution(13908447643258028780)
XLA Ops:
  0.0 115.4 %correlate.1 = bf16[512,2048]{1,0:T(8,128)(2,1)S(1)} custom-call(bf16[512,2048]{1,0:T(8,128)(2,1)} %bitcast.3, bf16[4,512,2048]{2,1,0:T(8,128)(2,1)} %constant.2.clone.tbl_hbm), custom_call_target="tpu_custom_call" | custom-call | tf_op jit(solution)/shard_map/correlate/pallas_call | solution.py:357
  115.4 1.3 %copy.4 = bf16[4,128,2048]{2,1,0:T(8,128)(2,1)} copy(bf16[4,128,2048]{2,1,0:T(8,128)(2,1)S(1)} %bitcast.2) | data formatting | bytes 4194304

commit v5 on v3

--- a/solution.py
+++ b/solution.py
@@ -286,8 +286,6 @@
         return carry
 
     lax.fori_loop(1, STAGES, middle, 0)
-    products(STAGES - 1)
-
     half = me // 8
 
     def lags(s, sides):
@@ -317,7 +315,11 @@
 
         lax.fori_loop(0, 4, tile, 0)
 
-    for s in range(STAGES - 1):
+    for s in range(1):
+        lags(s, (0, 1))
+    products(STAGES - 1)
+
+    for s in range(1, STAGES - 1):
         lags(s, (0, 1))
     lags(STAGES - 1, (1,))
     lags(STAGES - 1, (0,))

time: 117 us -> 117 us (level)
  no operation moved by 1% of the time
where the time goes in v5:
time: 117 us
  Pallas kernels  116 us (99%)
  local copies, waits for them, and re-layouts  1.32 us (1%)
    pallas_call x1, Pallas kernels, per_device(): pl.pallas_call(kernel, out_shape=pltpu.VMEM((rows, S), BF16), in_specs=[a...  116 us

profile of v5, /device:TPU:31, one launch (start us, length us, event | category | flops | bytes accessed | tf_op | source)
XLA Modules:
  0.0 117.0 jit_solution(4410413139655055555)
XLA Ops:
  0.0 115.7 %correlate.1 = bf16[512,2048]{1,0:T(8,128)(2,1)S(1)} custom-call(bf16[512,2048]{1,0:T(8,128)(2,1)} %bitcast.3, bf16[4,512,2048]{2,1,0:T(8,128)(2,1)} %constant.2.clone.tbl_hbm), custom_call_target="tpu_custom_call" | custom-call | tf_op jit(solution)/shard_map/correlate/pallas_call | solution.py:346
  115.7 1.3 %copy.4 = bf16[4,128,2048]{2,1,0:T(8,128)(2,1)} copy(bf16[4,128,2048]{2,1,0:T(8,128)(2,1)S(1)} %bitcast.2) | data formatting | bytes 4194304
